TPU v7x, 32 devices: a whole 2x2x4 slice. The times are simulated.
32 devices in a mesh: grp: 4 (over z), lat: 8 (over y, x, core).
Axes of the slice: x: 2, y: 2, z: 4, core: 2. Of those that a mesh axis runs over, the one named last changes fastest.
Arguments:
- stream: bfloat16 [256, 8192], P('lat'), may hold values from -26 to 26
- batch_index: int32 [256], replicated, may hold values from 0 to 255
- weight: bfloat16 [8192, 4096], P(None, ('grp', 'lat')), may hold values from -0.26516504 to 0.26516504
- enc_bias: float32 [4096], P(('grp', 'lat')), may hold values from -1.5 to 0.5
- dec_bias: float32 [8192], replicated, may hold values from -3 to 3
Outputs:
- weight_grad: bfloat16 [8192, 4096], P(None, ('grp', 'lat'))
- bias_grad: float32 [4096], P(('grp', 'lat'))
- recon_error: bfloat16 [256, 8192], P('lat')
All inputs are finite; a program needn't handle non-finite values.
Results may differ from a plain program's by a relative error of at most 0.025.
Values may be sent and summed in bfloat16 or wider, within the bound.
A program may use at most 64 MiB of HBM per device.

v0:
```python
import jax
import jax.numpy as jnp
from jax import lax
from jax.sharding import PartitionSpec as P

sharpness = 8.0
penalty = 0.25
epsilon = 1e-06


def body(stream, batch_index, weight, enc_bias, dec_bias):
    own_rows = stream.shape[0]
    rank_lat = lax.axis_index("lat")
    gathered = lax.all_gather(stream, "lat", axis=0, tiled=True)
    batch = jnp.take(gathered, batch_index, axis=0)
    centered = (batch.astype(jnp.float32) - dec_bias).astype(jnp.bfloat16)
    preact = jnp.dot(centered, weight, preferred_element_type=jnp.float32) + enc_bias
    active = (jax.nn.softplus(sharpness * preact) / sharpness).astype(jnp.bfloat16)
    first_row = rank_lat * own_rows
    own_batch = lax.dynamic_slice_in_dim(batch, first_row, own_rows, 0)
    block_recon = lax.psum_scatter(
        lax.dot_general(
            active, weight, (((1,), (1,)), ((), ())), preferred_element_type=jnp.float32
        ).astype(jnp.bfloat16),
        "lat",
        scatter_dimension=0,
        tiled=True,
    )
    recon = lax.psum(block_recon, "grp").astype(jnp.float32)
    error_own = recon + dec_bias - own_batch.astype(jnp.float32)
    grad_own = (2.0 * error_own).astype(jnp.bfloat16)
    grad_rows = lax.all_gather(grad_own, "lat", axis=0, tiled=True)
    grad_active = jnp.dot(grad_rows, weight, preferred_element_type=jnp.float32)
    decoder_grad = lax.dot_general(
        grad_rows, active, (((0,), (0,)), ((), ())), preferred_element_type=jnp.float32
    )
    grad_pre = (grad_active + penalty) * jax.nn.sigmoid(sharpness * preact)
    encoder_grad = lax.dot_general(
        centered,
        grad_pre.astype(jnp.bfloat16),
        (((0,), (0,)), ((), ())),
        preferred_element_type=jnp.float32,
    )
    grad_raw = encoder_grad + decoder_grad
    bias_raw = jnp.sum(grad_pre, axis=0)
    local_squares = jnp.sum(grad_raw * grad_raw) + jnp.sum(bias_raw * bias_raw)
    total_squares = lax.psum(local_squares, ("grp", "lat"))
    entries = (weight.shape[0] + 1) * weight.shape[1] * lax.axis_size("lat") * lax.axis_size("grp")
    factor = jnp.minimum(1.0, 1.0 / jnp.sqrt(total_squares / entries + epsilon))
    return (
        (grad_raw * factor).astype(jnp.bfloat16),
        bias_raw * factor,
        error_own.astype(jnp.bfloat16),
    )


def solution(mesh):
    return jax.shard_map(
        body,
        mesh=mesh,
        in_specs=(P("lat", None), P(), P(None, ("grp", "lat")), P(("grp", "lat")), P()),
        out_specs=(P(None, ("grp", "lat")), P(("grp", "lat")), P("lat", None)),
        check_vma=False,
    )
```

profile of v0, /device:TPU:0, one launch (start us, length us, event | category | flops | bytes accessed | tf_op | source)
XLA Modules:
  0.0 264.0 jit_solution(18357521309431948738)
XLA Ops:
  7.2 0.0 copy-start
  7.2 0.0 all-gather.3.cloned.1.call-start
  7.2 0.7 all-gather.3.cloned.1.call-update
  7.9 0.0 reduce-scatter.2.cloned.1.call-start
  8.0 0.7 compare_select_fusion.1
  8.7 0.7 compare_and_fusion
  9.3 40.0 %all-gather.3.cloned.1.call-done = bf16[256,8192]{1,0:T(8,128)(2,1)} async-done(((bf16[32,8192]{1,0:T(8,128)(2,1)}), bf16[256,8192]{1,0:T(8,128)(2,1)}) %all-gather.3.cloned.1.call-update) | async-done | bytes 4194320 | tf_op jit(solution)/shard_map/all_gather | solution.py:14
  49.4 11.7 %gather_fusion = bf16[256,8192]{1,0:T(8,128)(2,1)} fusion(bf16[256,8192]{1,0:T(8,128)(2,1)} %all-gather.3.cloned.1.call-done, s32[1024]{0:T(1024)S(1)} %pad_clamp_fusion), kind=kCustom, calls=%fused_computation | custom fusion | bytes 8389632 | tf_op jit(solution)/shard_map/jit(_take)/gather | solution.py:15
  61.0 0.0 copy-start.4
  61.0 0.0 copy-start.5
  61.0 2.7 %broadcast_select_fusion = bf16[256,8192]{1,0:T(8,128)(2,1)S(1)} fusion(bf16[256,8192]{1,0:T(8,128)(2,1)} %gather_fusion, pred[256]{0:T(512)(128)(4,1)S(1)} %compare_and_fusion), kind=kLoop, calls=%fused_computation.6 | loop fusion | flops 2097152 | bytes 8388864 | tf_op jit(solution)/shard_map/jit(_take)/select_n | solution.py:15
  63.7 0.0 copy-start.1
  63.7 1.9 copy-done.1
  65.7 0.0 copy-done
  65.7 0.0 copy-done.4
  65.7 0.0 copy-done.5
  65.7 1.3 fusion.4
  67.0 3.2 %convolution_convert_fusion = bf16[256,8192]{1,0:T(8,128)(2,1)} fusion(bf16[8192,128]{1,0:T(8,128)(2,1)S(1)} %copy-done, f32[256,128]{1,0:T(8,128)S(1)} %fusion.4), kind=kOutput, calls=%fused_computation.1 | convolution fusion | flops 539230208 | bytes 6422528 | tf_op jit(solution)/shard_map/dot_general | solution.py:22
  70.2 0.0 reduce-scatter.2.cloned.1.call-update
  70.2 0.0 all-reduce.2.cloned.1.call-start
  70.3 51.5 %reduce-scatter.2.cloned.1.call-done = bf16[32,8192]{1,0:T(8,128)(2,1)} async-done(((bf16[256,8192]{1,0:T(8,128)(2,1)}), bf16[32,8192]{1,0:T(8,128)(2,1)}) %reduce-scatter.2.cloned.1.call-update) | async-done | bytes 524304 | tf_op jit(solution)/shard_map/reduce_scatter | solution.py:21
  121.7 0.0 all-reduce.2.cloned.1.call-update
  121.8 0.2 all-gather.5.cloned.1.call-start
  122.0 40.5 %all-reduce.2.cloned.1.call-done = bf16[32,8192]{1,0:T(8,128)(2,1)} async-done(((bf16[32,8192]{1,0:T(8,128)(2,1)}), bf16[32,8192]{1,0:T(8,128)(2,1)}) %all-reduce.2.cloned.1.call-update) | async-done | bytes 524304 | tf_op jit(solution)/shard_map/psum | solution.py:29
  162.5 2.4 fusion.5
  164.9 0.0 all-gather.5.cloned.1.call-update
  164.9 36.9 %all-gather.5.cloned.1.call-done = bf16[256,8192]{1,0:T(8,128)(2,1)} async-done(((bf16[32,8192]{1,0:T(8,128)(2,1)}), bf16[256,8192]{1,0:T(8,128)(2,1)}) %all-gather.5.cloned.1.call-update) | async-done | bytes 4194320 | tf_op jit(solution)/shard_map/all_gather | solution.py:32
  201.8 0.0 copy-start.2
  201.8 3.6 %fusion.11 = (f32[128]{0:T(128)S(1)}, bf16[256,128]{1,0:T(8,128)(2,1)S(1)}) fusion(f32[256,128]{1,0:T(8,128)S(1)} %fusion.4, bf16[256,8192]{1,0:T(8,128)(2,1)} %all-gather.5.cloned.1.call-done, bf16[8192,128]{1,0:T(8,128)(2,1)S(1)} %copy-done), kind=kOutput, calls=%fused_computation.25 | convolution fusion | flops 537100160 | bytes 6488576 | tf_op jit(solution)/shard_map/dot_general | solution.py:33
  205.4 0.0 copy-done.2
  205.4 0.0 copy-start.3
  205.4 1.5 fusion
  206.9 0.6 multiply_reduce_fusion.1
  207.5 0.1 copy-done.3
  207.6 4.4 %multiply_reduce_fusion = (f32[]{:T(128)}, f32[8192,128]{1,0:T(8,128)}) fusion(f32[8192,128]{1,0:T(8,128)S(1)} %fusion, bf16[256,8192]{1,0:T(8,128)(2,1)S(1)} %copy-done.3, f32[256,128]{1,0:T(8,128)S(1)} %fusion.4), kind=kOutput, calls=%fused_computation.5 | convolution fusion | flops 540278784 | bytes 12713988 | tf_op jit(solution)/shard_map/dot_general | solution.py:34
  213.2 39.4 %psum.15 = f32[]{:T(128)} all-reduce(f32[]{:T(128)S(6)} %add.67), channel_id=1, replica_groups=mesh['grp'=4,'lat'=8] {'grp','lat'}, use_global_device_ids=true, to_apply=%region_5.6 | all-reduce | flops 1 | bytes 8 | tf_op jit(solution)/shard_map/psum | solution.py:47
  253.3 0.5 broadcast_multiply_fusion
  253.8 3.7 %multiply_convert_fusion = bf16[8192,128]{1,0:T(8,128)(2,1)} fusion(f32[8192,128]{1,0:T(8,128)} %get-tuple-element.6, f32[]{:T(128)S(6)} %min.3), kind=kLoop, calls=%fused_computation.4 | loop fusion | flops 2097152 | bytes 6291460 | tf_op jit(solution)/shard_map/convert_element_type | solution.py:51
  (1 shorter events, 0.0 us)
Async XLA Ops:
  7.2 58.5 %copy-start = (bf16[8192,128]{1,0:T(8,128)(2,1)S(1)}, bf16[8192,128]{1,0:T(8,128)(2,1)}, u32[]{:S(2)}) copy-start(bf16[8192,128]{1,0:T(8,128)(2,1)} %param.7) | copy-start | bytes 6291460
  7.2 42.2 %all-gather.3.cloned.1.call-start = ((), (), s32[]{:S(2)}) async-start(), calls=%async_computation.1 | async-start | bytes 4718592 | tf_op jit(solution)/shard_map/all_gather | solution.py:14
  7.9 113.8 %reduce-scatter.2.cloned.1.call-start = ((), (), s32[]{:S(2)}) async-start(), calls=%async_computation.2 | async-start | bytes 4718592 | tf_op jit(solution)/shard_map/reduce_scatter | solution.py:21
  61.0 4.6 %copy-start.4 = (f32[8192]{0:T(1024)S(1)}, f32[8192]{0:T(1024)}, u32[]{:S(2)}) copy-start(f32[8192]{0:T(1024)} %param.9) | copy-start | bytes 98308
  61.0 4.6 %copy-start.5 = (f32[128]{0:T(128)S(1)}, f32[128]{0:T(128)}, u32[]{:S(2)}) copy-start(f32[128]{0:T(128)} %param.8) | copy-start | bytes 1540
  63.7 1.9 copy-start.1
  70.2 92.3 %all-reduce.2.cloned.1.call-start = ((), (), s32[]{:S(2)}) async-start(), calls=%async_computation.3 | async-start | bytes 1048576 | tf_op jit(solution)/shard_map/psum | solution.py:29
  121.8 80.0 %all-gather.5.cloned.1.call-start = ((), (), s32[]{:S(2)}) async-start(), calls=%async_computation.4 | async-start | bytes 4718592 | tf_op jit(solution)/shard_map/all_gather | solution.py:32
  201.8 3.6 %copy-start.2 = (bf16[256,8192]{1,0:T(8,128)(2,1)S(1)}, bf16[256,8192]{1,0:T(8,128)(2,1)}, u32[]{:S(2)}) copy-start(bf16[256,8192]{1,0:T(8,128)(2,1)} %copy-done.1) | copy-start | bytes 12582916
  205.4 2.2 copy-start.3
Sparse Core Ops, SparseCore 0:
  9.9 39.4 all-gather.2
  70.4 51.3 reduce-scatter.1
  124.2 38.2 all-reduce.1
  165.0 36.6 all-gather.4
where the time goes:
time: 264 us
  waiting for transfers between devices  170 us (64%)
  blocking collectives  39.4 us (15%)
  between operations  15.8 us (6%)
  matrix products  14 us (5%)
  local copies, waits for them, and re-layouts  13.7 us (5%)
  other arithmetic  11.2 us (4%)
    reduce_scatter x1, waiting for transfers between devices, body(): lax.psum_scatter(lax.dot_general(active, weight, (((1,), (1,)), ((), ()))...  51.5 us
    psum x1, waiting for transfers between devices, body(): recon = lax.psum(block_recon, 'grp').astype(jnp.float32)  40.5 us
    all_gather x1, waiting for transfers between devices, body(): gathered = lax.all_gather(stream, 'lat', axis=0, tiled=True)  40 us
    psum x1, blocking collectives, body(): total_squares = lax.psum(local_squares, ('grp', 'lat'))  39.4 us
    all_gather x1, waiting for transfers between devices, body(): grad_rows = lax.all_gather(grad_own, 'lat', axis=0, tiled=True)  36.9 us
    gather x1, local copies, waits for them, and re-layouts, body(): batch = jnp.take(gathered, batch_index, axis=0)  11.7 us
  transfers between devices with their start and end apart: 4, of which 4 were waited for; matrix products, arithmetic and copies ran while one was open for 1% of the time, Pallas kernels for 0%

commit v1 on v0

v1 whole, which is shorter than its diff:
```python
import functools

import jax
import jax.numpy as jnp
from jax import lax
from jax.experimental import pallas as pl
from jax.experimental.pallas import tpu as pltpu
from jax.sharding import PartitionSpec as P

sharpness = 8.0
penalty = 0.25
epsilon = 1e-06
f32 = jnp.float32
bf16 = jnp.bfloat16
MESH = pl.DeviceIdType.MESH


def chunk_of(length, most):
    return next(c for c in range(min(most, length), 0, -16) if length % c == 0)


def bit_orders(n_lat, n_grp):
    lat_bits = n_lat.bit_length() - 1
    grp_bits = n_grp.bit_length() - 1
    x_bits = (lat_bits - 1) // 2
    core = [("lat", 1)]
    x = [("lat", 1 << b) for b in range(1, 1 + x_bits)]
    y = [("lat", 1 << b) for b in range(1 + x_bits, lat_bits)]
    z = [("grp", 1 << b) for b in range(grp_bits)]
    return core, x, y, z


def kernel(n_lat, n_grp, stream_ref, idx_row_ref, idx_col_ref, weight_ref, enc_ref, dec_ref,
           wgrad_ref, bias_ref, err_ref,
           gathered, centered_t, weight_t, part, landed, grad_t, raw, tiles,
           gs_sem, gr_sem, rs_sem, rr_sem, as_sem, ar_sem, ts_sem, tr_sem):
    rows, width = stream_ref.shape
    tokens = idx_row_ref.shape[1]
    n = n_lat * n_grp
    me = {"lat": lax.axis_index("lat"), "grp": lax.axis_index("grp")}
    core, x, y, z = bit_orders(n_lat, n_grp)
    everyone = core + x + y + z

    def partner(bit):
        axis, mask = bit
        return {a: (jnp.bitwise_xor(me[a], mask) if a == axis else me[a]) for a in ("grp", "lat")}

    def side(bit):
        axis, mask = bit
        return jnp.bitwise_and(jnp.right_shift(me[axis], mask.bit_length() - 1), 1)

    def send(src, dst, send_sem, recv_sem, bit):
        copy = pltpu.make_async_remote_copy(
            src_ref=src, dst_ref=dst, send_sem=send_sem, recv_sem=recv_sem,
            device_id=partner(bit), device_id_type=MESH)
        copy.start()
        return copy

    barrier = pltpu.get_barrier_semaphore()
    for bit in everyone:
        pl.semaphore_signal(barrier, inc=1, device_id=partner(bit), device_id_type=MESH)
    pl.semaphore_wait(barrier, len(everyone))

    half = width // 2
    flows = []
    for p, order in enumerate((x + y + core, y + x + core)):
        flows.append((pl.ds(p * half, half), [mask for _, mask in order]))
    gathers = [{}, {}]

    def forward(p, m, later):
        cols, order = flows[p]
        rank = jnp.bitwise_xor(me["lat"], m)
        src = stream_ref.at[:, cols] if m == 0 else gathered.at[rank, :, cols]
        for mask in later:
            gathers[p][m | mask] = send(
                src, gathered.at[rank, :, cols], gs_sem.at[p, m | mask], gr_sem.at[p, m | mask], ("lat", mask))

    span = [0]
    for p in (0, 1):
        forward(p, 0, flows[p][1])
    own_copy = pltpu.make_async_copy(stream_ref, gathered.at[me["lat"]], gs_sem.at[0, 0])
    own_copy.start()

    c = chunk_of(width, 512)
    for at in range(0, width, c):
        weight_t[:, at:at + c] = weight_ref[at:at + c, :].T
    square = (tokens, tokens)
    hits = (lax.broadcasted_iota(jnp.int32, square, 0) == idx_row_ref[...]).astype(f32)
    count = jnp.sum(hits, axis=1, keepdims=True)

    spans = [[0], [0]]
    for stage in range(len(flows[0][1])):
        fresh = []
        for p in (0, 1):
            order = flows[p][1]
            for m in spans[p]:
                fresh.append((p, m | order[stage]))
        for p, m in fresh:
            gathers[p][m].wait_recv()
            forward(p, m, flows[p][1][stage + 1:])
            spans[p].append(m)
    own_copy.wait()

    preact = jnp.zeros((tokens, weight_ref.shape[1]), f32)

    def center(at, c):
        block = gathered[:, :, at:at + c].astype(f32).reshape(tokens, c)
        return (block - dec_ref[:, at:at + c]).astype(bf16)

    for at in range(0, width, c):
        preact = preact + jnp.dot(center(at, c), weight_ref[at:at + c, :], preferred_element_type=f32)
    preact = preact + enc_ref[...]
    sharp = sharpness * preact
    active32 = (jnp.maximum(sharp, 0.0) + jnp.log1p(jnp.exp(-jnp.abs(sharp)))) / sharpness
    active = active32.astype(bf16)

    units = width // (16 * n)
    if units >= 8:
        small = units // 4
        big = (units - small) // 2
        small = units - 2 * big
        parts = [(big, core + x + y + z), (big, core + y + x + z), (small, core + z + x + y)]
    else:
        parts = [(units, core + x + y + z)]
    base, plan = 0, []
    for size, order in parts:
        plan.append((base, size * 16 * n, order))
        base += size * 16 * n
    n_bits = len(everyone)

    def aligned(at):
        return pl.multiple_of(at, 16)

    def term(at, length):
        c = chunk_of(length, 512)
        for k in range(0, length, c):
            here = pl.ds(aligned(at + k), c)
            part[here, :] = lax.dot_general(
                weight_ref[here, :], active, (((1,), (1,)), ((), ())), preferred_element_type=f32).astype(bf16)

    def over(length, most, step):
        c = chunk_of(length, most)
        if length == c:
            step(0, c)
        else:
            @pl.loop(0, length // c)
            def _(k):
                step(aligned(k * c), c)

    where, room = [], 0
    sends = []
    copies = {}
    for p, (start, length, order) in enumerate(plan):
        stay = aligned(start + side(order[0]) * (length // 2))
        go = aligned(start + (1 - side(order[0])) * (length // 2))
        term(go, length // 2)
        spot = room
        room += length // 2
        copies[p] = send(part.at[pl.ds(go, length // 2), :], landed.at[pl.ds(spot, length // 2), :],
                         rs_sem.at[p, 0], rr_sem.at[p, 0], order[0])
        sends.append(copies[p])
        where.append([stay, length // 2, spot])
    for p in range(len(plan)):
        term(where[p][0], where[p][1])

    for stage in range(1, n_bits):
        for p, (_, _, order) in enumerate(plan):
            at, length, spot = where[p]
            copies[p].wait_recv()
            now = length // 2
            stay_by = side(order[stage]) * now
            go_by = (1 - side(order[stage])) * now

            def add(by):
                def step(k, c):
                    here = pl.ds(aligned(at + by + k), c)
                    part[here, :] = (part[here, :].astype(f32)
                                     + landed[pl.ds(aligned(spot + by + k), c), :].astype(f32)).astype(bf16)
                over(now, 128, step)

            add(go_by)
            next_spot = room
            room += now
            copies[p] = send(part.at[pl.ds(aligned(at + go_by), now), :], landed.at[pl.ds(next_spot, now), :],
                             rs_sem.at[p, stage], rr_sem.at[p, stage], order[stage])
            sends.append(copies[p])
            add(stay_by)
            where[p] = [aligned(at + stay_by), now, next_spot]
        if stage == 1:
            for k in range(0, width, c):
                centered_t[k:k + c, :] = center(k, c).T

    for p, (_, _, order) in enumerate(plan):
        at, length, spot = where[p]
        copies[p].wait_recv()

        def finish(k, c):
            here = pl.ds(aligned(at + k), c)
            total = part[here, :].astype(f32) + landed[pl.ds(aligned(spot + k), c), :].astype(f32)
            grad_t[here, :] = (2.0 * (total - centered_t[here, :].astype(f32))).astype(bf16)
        over(length, 128, finish)

    for stage in reversed(range(n_bits)):
        for p, (_, _, order) in enumerate(plan):
            at, length, _ = where[p]
            if stage < n_bits - 1:
                copies[p].wait_recv()
            region = grad_t.at[pl.ds(at, length), :]
            copies[p] = send(region, region, as_sem.at[p, stage], ar_sem.at[p, stage], order[stage])
            sends.append(copies[p])
            where[p] = [aligned(at - side(order[stage]) * length), 2 * length, 0]
    for p in range(len(plan)):
        copies[p].wait_recv()

    grad_active_t = jnp.zeros((weight_ref.shape[1], tokens), f32)
    for k in range(0, width, c):
        grad_active_t = grad_active_t + jnp.dot(weight_t[:, k:k + c], grad_t[k:k + c, :], preferred_element_type=f32)
    grad_pre = (grad_active_t.T + penalty) * jax.nn.sigmoid(sharp) * count
    bias_raw = jnp.sum(grad_pre, axis=0, keepdims=True)
    pre16 = grad_pre.astype(bf16)
    drawn = (active32 * count).astype(bf16)
    squares = jnp.zeros((8, weight_ref.shape[1]), f32)
    for k in range(0, width, c):
        block = (jnp.dot(centered_t[k:k + c, :], pre16, preferred_element_type=f32)
                 + jnp.dot(grad_t[k:k + c, :], drawn, preferred_element_type=f32))
        raw[k:k + c, :] = block
        squares = squares + jnp.sum((block * block).reshape(c // 8, 8, block.shape[1]), axis=0)
    first = lax.broadcasted_iota(jnp.int32, squares.shape, 0) == 0
    squares = squares + jnp.where(first, bias_raw * bias_raw, 0.0)

    tiles[0] = squares
    own = idx_col_ref[pl.ds(pl.multiple_of(me["lat"] * rows, 8), rows), :]
    pick = (lax.broadcasted_iota(jnp.int32, (rows, tokens), 1) == own).astype(bf16)
    for i, bit in enumerate(everyone):
        copy = send(tiles.at[2 * i], tiles.at[2 * i + 1], ts_sem.at[i], tr_sem.at[i], bit)
        sends.append(copy)
        if i == 0:
            for k in range(0, width, c):
                rows_of = lax.dot_general(pick, grad_t[k:k + c, :], (((1,), (1,)), ((), ())), preferred_element_type=f32)
                err_ref[:, k:k + c] = (0.5 * rows_of).astype(bf16)
        copy.wait_recv()
        tiles[2 * i + 2] = tiles[2 * i] + tiles[2 * i + 1]
    total = jnp.sum(tiles[2 * n_bits])
    entries = (width + 1) * weight_ref.shape[1] * n
    mean = jnp.full((1, weight_ref.shape[1]), total / entries + epsilon, f32)
    factor = jnp.minimum(1.0, 1.0 / jnp.sqrt(mean))
    bias_ref[...] = bias_raw * factor
    for k in range(0, width, c):
        wgrad_ref[k:k + c, :] = (raw[k:k + c, :] * factor).astype(bf16)

    for copy in sends:
        copy.wait_send()
    for p in (0, 1):
        for m in sorted(gathers[p]):
            gathers[p][m].wait_send()


def body(n_lat, n_grp, stream, batch_index, weight, enc_bias, dec_bias):
    rows, width = stream.shape
    tokens = batch_index.shape[0]
    latents = weight.shape[1]
    n_bits = (n_lat * n_grp).bit_length() - 1
    vmem = pl.BlockSpec(memory_space=pltpu.VMEM)
    dma = pltpu.SemaphoreType.DMA
    weight_grad, bias_grad, error = pl.pallas_call(
        functools.partial(kernel, n_lat, n_grp),
        out_shape=(
            jax.ShapeDtypeStruct(weight.shape, bf16),
            jax.ShapeDtypeStruct((1, latents), f32),
            jax.ShapeDtypeStruct((rows, width), bf16),
        ),
        in_specs=[vmem] * 6,
        out_specs=(vmem, vmem, vmem),
        scratch_shapes=[
            pltpu.VMEM((n_lat, rows, width), bf16),
            pltpu.VMEM((width, tokens), bf16),
            pltpu.VMEM((latents, width), bf16),
            pltpu.VMEM((width, tokens), bf16),
            pltpu.VMEM((width, tokens), bf16),
            pltpu.VMEM((width, tokens), bf16),
            pltpu.VMEM((width, latents), f32),
            pltpu.VMEM((2 * n_bits + 1, 8, latents), f32),
            dma((2, n_lat)),
            dma((2, n_lat)),
            dma((3, n_bits)),
            dma((3, n_bits)),
            dma((3, n_bits)),
            dma((3, n_bits)),
            dma((n_bits,)),
            dma((n_bits,)),
        ],
        compiler_params=pltpu.CompilerParams(
            collective_id=0, has_side_effects=True, vmem_limit_bytes=56 * 1024 * 1024),
        cost_estimate=pl.CostEstimate(
            flops=2 * tokens * width * latents * 5, bytes_accessed=8 * width * latents, transcendentals=0),
    )(
        stream,
        batch_index.reshape(1, tokens),
        batch_index.reshape(tokens, 1),
        weight,
        enc_bias.reshape(1, latents),
        dec_bias.reshape(1, width),
    )
    return weight_grad, bias_grad.reshape(latents), error


def solution(mesh):
    return jax.shard_map(
        functools.partial(body, mesh.shape["lat"], mesh.shape["grp"]),
        mesh=mesh,
        in_specs=(P("lat", None), P(), P(None, ("grp", "lat")), P(("grp", "lat")), P()),
        out_specs=(P(None, ("grp", "lat")), P(("grp", "lat")), P("lat", None)),
        check_vma=False,
    )
```

time: 264 us -> 107 us (0.41)
  waiting for transfers between devices: 170 us -> 0 us
  Pallas kernels: 0 us -> 101 us
  blocking collectives: 39.4 us -> 0 us
  between operations: 15.8 us -> 0.66 us
  matrix products: 14 us -> 0 us
  other arithmetic: 11.2 us -> 0 us
  local copies, waits for them, and re-layouts: 13.7 us -> 5.89 us
    pallas_call x0 -> x1, Pallas kernels: none -> 101 us  [body(): pl.pallas_call(functools.partial(kernel, n_lat, n_grp), out_shape=(jax.Sh...]
    all_gather x2 -> x0, waiting for transfers between devices: 76.9 us -> none  [the longest x1 40 us: body(): gathered = lax.all_gather(stream, 'lat', axis=0, tiled=True)]
    reduce_scatter x1 -> x0, waiting for transfers between devices: 51.5 us -> none  [body(): lax.psum_scatter(lax.dot_general(active, weight, (((1,), (1,)), ((), ()))...]
    psum x1 -> x0, waiting for transfers between devices: 40.5 us -> none  [body(): recon = lax.psum(block_recon, 'grp').astype(jnp.float32)]
    psum x1 -> x0, blocking collectives: 39.4 us -> none  [body(): total_squares = lax.psum(local_squares, ('grp', 'lat'))]
    dot_general x5 -> x0, matrix products: 14 us -> none  [the longest x1 4.35 us: body(): lax.dot_general(grad_rows, active, (((0,), (0,)), ((), ())), preferred_el...]
    gather x1 -> x0, local copies, waits for them, and re-layouts: 11.7 us -> none  [body(): batch = jnp.take(gathered, batch_index, axis=0)]
    convert_element_type x2 -> x0, other arithmetic: 6.09 us -> none  [the longest x1 3.72 us: body(): (grad_raw * factor).astype(jnp.bfloat16)]
  transfers between devices with their start and end apart: 4 -> 0, of which waited for: 4 -> 0; matrix products, arithmetic and copies ran while one was open for 1% -> 0% of each run, Pallas kernels for 0% -> 0%
where the time goes in v1:
time: 107 us
  Pallas kernels  101 us (94%)
  local copies, waits for them, and re-layouts  5.89 us (6%)
    pallas_call x1, Pallas kernels, body(): pl.pallas_call(functools.partial(kernel, n_lat, n_grp), out_shape=(jax.Sh...  101 us
    unnamed x7, local copies, waits for them, and re-layouts  4.42 us

profile of v1, /device:TPU:0, one launch (start us, length us, event | category | flops | bytes accessed | tf_op | source)
XLA Modules:
  0.0 107.1 jit_solution(8582749155968547272)
XLA Ops:
  0.6 1.5 %copy.8.idx_col_ref = s32[256,1]{1,0:T(8,128)} copy(s32[256,1]{0,1:T(1,128)} %bitcast.5) | data formatting | bytes 2048 | tf_op jit(solution)/shard_map/reshape | solution.py:299
  2.1 100.5 %shard_map.76 = (bf16[8192,128]{1,0:T(8,128)(2,1)}, f32[1,128]{1,0:T(1,128)}, bf16[32,8192]{1,0:T(8,128)(2,1)}) custom-call(bf16[32,8192]{1,0:T(8,128)(2,1)} %stream_ref.1, s32[1,256]{1,0:T(1,128)} %bitcast.6, s32[256,1]{1,0:T(8,128)} %copy.8.idx_col_ref, bf16[8192,128]{1,0:T(8,128)(2,1)} %weight_ref.1, f32[1,128]{1,0:T(1,128)} %bitcast.8, f32[1,8192]{1,0:T(1,128)} %bitcast.7), custom_call_target="tpu_custom_call" | custom-call | flops 2684354560 | bytes 8388608 | tf_op jit(solution)/shard_map/pallas_call | solution.py:265
  102.7 0.0 copy-start.1
  102.7 0.0 copy-start
  102.7 3.1 %copy.12 = bf16[8192,128]{1,0:T(8,128)(2,1)} copy(bf16[8192,128]{1,0:T(8,128)(2,1)} %get-tuple-element.12) | data formatting | bytes 4194304
  105.8 0.0 copy-done.1
  105.8 0.5 copy.13
  106.3 0.0 copy-done
  106.3 0.8 copy.14
Async XLA Ops:
  102.7 3.1 %copy-start.1 = (f32[1,128]{1,0:T(1,128)S(1)}, f32[1,128]{1,0:T(1,128)}, u32[]{:S(2)}) copy-start(f32[1,128]{1,0:T(1,128)} %get-tuple-element.7) | copy-start | bytes 1540
  102.7 3.6 %copy-start = (bf16[32,8192]{1,0:T(8,128)(2,1)S(1)}, bf16[32,8192]{1,0:T(8,128)(2,1)}, u32[]{:S(2)}) copy-start(bf16[32,8192]{1,0:T(8,128)(2,1)} %get-tuple-element.14) | copy-start | bytes 1572868

commit v2 on v1

--- a/solution.py
+++ b/solution.py
@@ -30,12 +30,19 @@
     return core, x, y, z
 
 
-def kernel(n_lat, n_grp, stream_ref, idx_row_ref, idx_col_ref, weight_ref, enc_ref, dec_ref,
-           wgrad_ref, bias_ref, err_ref,
-           gathered, centered_t, weight_t, part, landed, grad_t, raw, tiles,
-           gs_sem, gr_sem, rs_sem, rr_sem, as_sem, ar_sem, ts_sem, tr_sem):
+def split(units, core, x, y, z):
+    if units < 16:
+        return [(units, core + x + y + z)]
+    once = [(3, core + x + y + z), (3, core + y + x + z), (2, core + z + x + y)]
+    return [(size * units // 16, order) for size, order in once * 2]
+
+
+def kernel(n_lat, n_grp, n_parts, stream_ref, idx_ref, weight_ref, enc_ref, dec_ref,
+           raw_ref, bias_ref, factor_ref, err_ref,
+           gathered, centered, centered_t, weight_t, part, landed, grad_t, raw, hits_t, lat_tiles, grp_tiles,
+           gs_sem, gr_sem, rs_sem, rr_sem, as_sem, ar_sem, ls_sem, lr_sem, zs_sem, zr_sem, out_sem):
     rows, width = stream_ref.shape
-    tokens = idx_row_ref.shape[1]
+    tokens = idx_ref.shape[1]
     n = n_lat * n_grp
     me = {"lat": lax.axis_index("lat"), "grp": lax.axis_index("grp")}
     core, x, y, z = bit_orders(n_lat, n_grp)
@@ -57,9 +64,10 @@
         return copy
 
     barrier = pltpu.get_barrier_semaphore()
-    for bit in everyone:
+    peers = [("lat", m) for m in range(1, n_lat)] + [("grp", m) for m in range(1, n_grp)]
+    for bit in peers:
         pl.semaphore_signal(barrier, inc=1, device_id=partner(bit), device_id_type=MESH)
-    pl.semaphore_wait(barrier, len(everyone))
+    pl.semaphore_wait(barrier, len(peers))
 
     half = width // 2
     flows = []
@@ -75,53 +83,59 @@
             gathers[p][m | mask] = send(
                 src, gathered.at[rank, :, cols], gs_sem.at[p, m | mask], gr_sem.at[p, m | mask], ("lat", mask))
 
-    span = [0]
     for p in (0, 1):
         forward(p, 0, flows[p][1])
-    own_copy = pltpu.make_async_copy(stream_ref, gathered.at[me["lat"]], gs_sem.at[0, 0])
-    own_copy.start()
 
     c = chunk_of(width, 512)
     for at in range(0, width, c):
         weight_t[:, at:at + c] = weight_ref[at:at + c, :].T
     square = (tokens, tokens)
-    hits = (lax.broadcasted_iota(jnp.int32, square, 0) == idx_row_ref[...]).astype(f32)
+    hits = (lax.broadcasted_iota(jnp.int32, square, 0) == idx_ref[...]).astype(f32)
     count = jnp.sum(hits, axis=1, keepdims=True)
-
+    hits_t[...] = hits.T
+
+    def center(m):
+        rank = jnp.bitwise_xor(me["lat"], m)
+        for at in range(0, width, c):
+            block = stream_ref[:, at:at + c] if m == 0 else gathered[rank, :, at:at + c]
+            centered[rank, :, at:at + c] = (block.astype(f32) - dec_ref[:, at:at + c]).astype(bf16)
+
+    def centered_chunk(at, c):
+        block = centered[:, :, at:at + c]
+        if rows % 16:
+            return block.astype(f32).reshape(tokens, c).astype(bf16)
+        return block.reshape(tokens, c)
+
+    center(0)
     spans = [[0], [0]]
     for stage in range(len(flows[0][1])):
         fresh = []
         for p in (0, 1):
-            order = flows[p][1]
             for m in spans[p]:
-                fresh.append((p, m | order[stage]))
+                fresh.append((p, m | flows[p][1][stage]))
+        fresh.sort(key=lambda pm: spans[pm[0]].index(pm[1] - flows[pm[0]][1][stage]))
+        complete = []
         for p, m in fresh:
             gathers[p][m].wait_recv()
             forward(p, m, flows[p][1][stage + 1:])
             spans[p].append(m)
-    own_copy.wait()
+            if m in spans[1 - p]:
+                if stage == len(flows[0][1]) - 1:
+                    center(m)
+                else:
+                    complete.append(m)
+        for m in complete:
+            center(m)
 
     preact = jnp.zeros((tokens, weight_ref.shape[1]), f32)
-
-    def center(at, c):
-        block = gathered[:, :, at:at + c].astype(f32).reshape(tokens, c)
-        return (block - dec_ref[:, at:at + c]).astype(bf16)
-
     for at in range(0, width, c):
-        preact = preact + jnp.dot(center(at, c), weight_ref[at:at + c, :], preferred_element_type=f32)
+        preact = preact + jnp.dot(centered_chunk(at, c), weight_ref[at:at + c, :], preferred_element_type=f32)
     preact = preact + enc_ref[...]
     sharp = sharpness * preact
     active32 = (jnp.maximum(sharp, 0.0) + jnp.log1p(jnp.exp(-jnp.abs(sharp)))) / sharpness
     active = active32.astype(bf16)
 
-    units = width // (16 * n)
-    if units >= 8:
-        small = units // 4
-        big = (units - small) // 2
-        small = units - 2 * big
-        parts = [(big, core + x + y + z), (big, core + y + x + z), (small, core + z + x + y)]
-    else:
-        parts = [(units, core + x + y + z)]
+    parts = split(width // (16 * n), core, x, y, z)
     base, plan = 0, []
     for size, order in parts:
         plan.append((base, size * 16 * n, order))
@@ -163,6 +177,12 @@
     for p in range(len(plan)):
         term(where[p][0], where[p][1])
 
+    def turn(stage):
+        total = width // c
+        for k in range(stage * total // n_bits * c, (stage + 1) * total // n_bits * c, c):
+            centered_t[k:k + c, :] = centered_chunk(k, c).T
+
+    turn(0)
     for stage in range(1, n_bits):
         for p, (_, _, order) in enumerate(plan):
             at, length, spot = where[p]
@@ -186,9 +206,7 @@
             sends.append(copies[p])
             add(stay_by)
             where[p] = [aligned(at + stay_by), now, next_spot]
-        if stage == 1:
-            for k in range(0, width, c):
-                centered_t[k:k + c, :] = center(k, c).T
+        turn(stage)
 
     for p, (_, _, order) in enumerate(plan):
         at, length, spot = where[p]
@@ -208,13 +226,21 @@
             region = grad_t.at[pl.ds(at, length), :]
             copies[p] = send(region, region, as_sem.at[p, stage], ar_sem.at[p, stage], order[stage])
             sends.append(copies[p])
-            where[p] = [aligned(at - side(order[stage]) * length), 2 * length, 0]
-    for p in range(len(plan)):
-        copies[p].wait_recv()
+            if stage > 0:
+                where[p] = [aligned(at - side(order[stage]) * length), 2 * length, 0]
 
     grad_active_t = jnp.zeros((weight_ref.shape[1], tokens), f32)
-    for k in range(0, width, c):
-        grad_active_t = grad_active_t + jnp.dot(weight_t[:, k:k + c], grad_t[k:k + c, :], preferred_element_type=f32)
+    for other in (False, True):
+        for p, (start, length, order) in enumerate(plan):
+            if other:
+                copies[p].wait_recv()
+            now = length // 2
+            at = start + (1 - side(order[0]) if other else side(order[0])) * now
+            c2 = chunk_of(now, 1024)
+            for k in range(0, now, c2):
+                here = pl.ds(pl.multiple_of(at + k, 128), c2)
+                grad_active_t = grad_active_t + jnp.dot(
+                    weight_t[:, here], grad_t[here, :], preferred_element_type=f32)
     grad_pre = (grad_active_t.T + penalty) * jax.nn.sigmoid(sharp) * count
     bias_raw = jnp.sum(grad_pre, axis=0, keepdims=True)
     pre16 = grad_pre.astype(bf16)
@@ -223,31 +249,46 @@
     for k in range(0, width, c):
         block = (jnp.dot(centered_t[k:k + c, :], pre16, preferred_element_type=f32)
                  + jnp.dot(grad_t[k:k + c, :], drawn, preferred_element_type=f32))
-        raw[k:k + c, :] = block
+        raw[k:k + c, :] = block.astype(bf16)
         squares = squares + jnp.sum((block * block).reshape(c // 8, 8, block.shape[1]), axis=0)
     first = lax.broadcasted_iota(jnp.int32, squares.shape, 0) == 0
     squares = squares + jnp.where(first, bias_raw * bias_raw, 0.0)
 
-    tiles[0] = squares
-    own = idx_col_ref[pl.ds(pl.multiple_of(me["lat"] * rows, 8), rows), :]
-    pick = (lax.broadcasted_iota(jnp.int32, (rows, tokens), 1) == own).astype(bf16)
-    for i, bit in enumerate(everyone):
-        copy = send(tiles.at[2 * i], tiles.at[2 * i + 1], ts_sem.at[i], tr_sem.at[i], bit)
-        sends.append(copy)
-        if i == 0:
-            for k in range(0, width, c):
-                rows_of = lax.dot_general(pick, grad_t[k:k + c, :], (((1,), (1,)), ((), ())), preferred_element_type=f32)
-                err_ref[:, k:k + c] = (0.5 * rows_of).astype(bf16)
+    lat_tiles[me["lat"]] = squares
+    arrivals = []
+    for m in range(1, n_lat):
+        slot = lat_tiles.at[me["lat"]]
+        arrivals.append(send(slot, slot, ls_sem.at[m], lr_sem.at[m], ("lat", m)))
+    out_copy = pltpu.make_async_copy(raw, raw_ref, out_sem)
+    out_copy.start()
+
+    pick = hits_t[pl.ds(pl.multiple_of(me["lat"] * rows, 8), rows), :].astype(bf16)
+
+    def recon(ks):
+        for k in ks:
+            rows_of = lax.dot_general(pick, grad_t[k:k + c, :], (((1,), (1,)), ((), ())), preferred_element_type=f32)
+            err_ref[:, k:k + c] = (0.5 * rows_of).astype(bf16)
+
+    recon(range(0, half, c))
+    for copy in arrivals:
         copy.wait_recv()
-        tiles[2 * i + 2] = tiles[2 * i] + tiles[2 * i + 1]
-    total = jnp.sum(tiles[2 * n_bits])
+    sends += arrivals
+    grp_tiles[me["grp"]] = jnp.sum(lat_tiles[...], axis=0)
+    arrivals = []
+    for m in range(1, n_grp):
+        slot = grp_tiles.at[me["grp"]]
+        arrivals.append(send(slot, slot, zs_sem.at[m], zr_sem.at[m], ("grp", m)))
+    recon(range(half, width, c))
+    for copy in arrivals:
+        copy.wait_recv()
+    sends += arrivals
+    total = jnp.sum(grp_tiles[...])
     entries = (width + 1) * weight_ref.shape[1] * n
     mean = jnp.full((1, weight_ref.shape[1]), total / entries + epsilon, f32)
-    factor = jnp.minimum(1.0, 1.0 / jnp.sqrt(mean))
-    bias_ref[...] = bias_raw * factor
-    for k in range(0, width, c):
-        wgrad_ref[k:k + c, :] = (raw[k:k + c, :] * factor).astype(bf16)
-
+    factor_ref[...] = jnp.minimum(1.0, 1.0 / jnp.sqrt(mean))
+    bias_ref[...] = bias_raw
+
+    out_copy.wait()
     for copy in sends:
         copy.wait_send()
     for p in (0, 1):
@@ -260,34 +301,42 @@
     tokens = batch_index.shape[0]
     latents = weight.shape[1]
     n_bits = (n_lat * n_grp).bit_length() - 1
+    n_parts = len(split(width // (16 * n_lat * n_grp), *bit_orders(n_lat, n_grp)))
     vmem = pl.BlockSpec(memory_space=pltpu.VMEM)
     dma = pltpu.SemaphoreType.DMA
-    weight_grad, bias_grad, error = pl.pallas_call(
-        functools.partial(kernel, n_lat, n_grp),
+    raw, bias_raw, factor, error = pl.pallas_call(
+        functools.partial(kernel, n_lat, n_grp, n_parts),
         out_shape=(
             jax.ShapeDtypeStruct(weight.shape, bf16),
             jax.ShapeDtypeStruct((1, latents), f32),
+            jax.ShapeDtypeStruct((1, latents), f32),
             jax.ShapeDtypeStruct((rows, width), bf16),
         ),
-        in_specs=[vmem] * 6,
-        out_specs=(vmem, vmem, vmem),
+        in_specs=[vmem] * 5,
+        out_specs=(pl.BlockSpec(memory_space=pl.ANY), vmem, vmem, vmem),
         scratch_shapes=[
+            pltpu.VMEM((n_lat, rows, width), bf16),
             pltpu.VMEM((n_lat, rows, width), bf16),
             pltpu.VMEM((width, tokens), bf16),
             pltpu.VMEM((latents, width), bf16),
             pltpu.VMEM((width, tokens), bf16),
             pltpu.VMEM((width, tokens), bf16),
             pltpu.VMEM((width, tokens), bf16),
-            pltpu.VMEM((width, latents), f32),
-            pltpu.VMEM((2 * n_bits + 1, 8, latents), f32),
+            pltpu.VMEM((width, latents), bf16),
+            pltpu.VMEM((tokens, tokens), f32),
+            pltpu.VMEM((n_lat, 8, latents), f32),
+            pltpu.VMEM((n_grp, 8, latents), f32),
             dma((2, n_lat)),
             dma((2, n_lat)),
-            dma((3, n_bits)),
-            dma((3, n_bits)),
-            dma((3, n_bits)),
-            dma((3, n_bits)),
-            dma((n_bits,)),
-            dma((n_bits,)),
+            dma((n_parts, n_bits)),
+            dma((n_parts, n_bits)),
+            dma((n_parts, n_bits)),
+            dma((n_parts, n_bits)),
+            dma((n_lat,)),
+            dma((n_lat,)),
+            dma((n_grp,)),
+            dma((n_grp,)),
+            dma,
         ],
         compiler_params=pltpu.CompilerParams(
             collective_id=0, has_side_effects=True, vmem_limit_bytes=56 * 1024 * 1024),
@@ -296,12 +345,12 @@
     )(
         stream,
         batch_index.reshape(1, tokens),
-        batch_index.reshape(tokens, 1),
         weight,
         enc_bias.reshape(1, latents),
         dec_bias.reshape(1, width),
     )
-    return weight_grad, bias_grad.reshape(latents), error
+    weight_grad = (raw.astype(f32) * factor).astype(bf16)
+    return weight_grad, (bias_raw * factor).reshape(latents), error
 
 
 def solution(mesh):

time: 107 us -> 96.6 us (0.903)
  Pallas kernels: 101 us -> 91.1 us
  local copies, waits for them, and re-layouts: 5.89 us -> 0.81 us
  other arithmetic: 0 us -> 3.89 us
    pallas_call x1, Pallas kernels: 101 us -> 91.1 us  [body(): pl.pallas_call(functools.partial(kernel, n_lat, n_grp, n_parts), out_shap...]
    unnamed x7, local copies, waits for them, and re-layouts: 4.42 us -> 0.81 us
    convert_element_type x0 -> x1, other arithmetic: none -> 3.38 us  [body(): weight_grad = (raw.astype(f32) * factor).astype(bf16)]
    reshape x1 -> x0, local copies, waits for them, and re-layouts: 1.47 us -> none  [body(): batch_index.reshape(tokens, 1)]
where the time goes in v2:
time: 96.6 us; the launch traced here: 96.4 us
  Pallas kernels  91.1 us (94%)
  other arithmetic  3.89 us (4%)
    pallas_call x1, Pallas kernels, body(): pl.pallas_call(functools.partial(kernel, n_lat, n_grp, n_parts), out_shap...  91.1 us
    convert_element_type x1, other arithmetic, body(): weight_grad = (raw.astype(f32) * factor).astype(bf16)  3.38 us

profile of v2, /device:TPU:0, one launch (start us, length us, event | category | flops | bytes accessed | tf_op | source)
XLA Modules:
  0.0 96.4 jit_solution(11530752052202985311)
XLA Ops:
  0.6 91.1 %shard_map.76 = (bf16[8192,128]{1,0:T(8,128)(2,1)}, f32[1,128]{1,0:T(1,128)}, f32[1,128]{1,0:T(1,128)}, bf16[32,8192]{1,0:T(8,128)(2,1)}) custom-call(bf16[32,8192]{1,0:T(8,128)(2,1)} %stream_ref.1, s32[1,256]{1,0:T(1,128)} %bitcast.8, bf16[8192,128]{1,0:T(8,128)(2,1)} %weight_ref.1, f32[1,128]{1,0:T(1,128)} %bitcast.9, f32[1,8192]{1,0:T(1,128)} %bitcast.7), custom_call_target="tpu_custom_call" | custom-call | flops 2684354560 | bytes 8388608 | tf_op jit(solution)/shard_map/pallas_call | solution.py:307
  91.7 0.0 copy-start.1
  91.7 0.0 copy-start.2
  91.7 0.0 copy-start
  91.7 3.4 %multiply_convert_fusion = bf16[8192,128]{1,0:T(8,128)(2,1)} fusion(bf16[8192,128]{1,0:T(8,128)(2,1)} %get-tuple-element.7, f32[128]{0:T(128)} %bitcast.6), kind=kLoop, calls=%fused_computation | loop fusion | flops 3145728 | bytes 4194816 | tf_op jit(solution)/shard_map/convert_element_type | solution.py:352
  95.1 0.0 copy-done.1
  95.1 0.0 copy-done.2
  95.1 0.5 multiply_bitcast_fusion
  95.6 0.0 copy-done
  95.6 0.8 copy.9
Async XLA Ops:
  91.7 3.4 %copy-start.1 = (f32[1,128]{1,0:T(1,128)S(1)}, f32[1,128]{1,0:T(1,128)}, u32[]{:S(2)}) copy-start(f32[1,128]{1,0:T(1,128)} %get-tuple-element.8) | copy-start | bytes 1540
  91.7 3.4 %copy-start.2 = (f32[1,128]{1,0:T(1,128)S(1)}, f32[1,128]{1,0:T(1,128)}, u32[]{:S(2)}) copy-start(f32[1,128]{1,0:T(1,128)} %get-tuple-element.9) | copy-start | bytes 1540
  91.7 3.9 %copy-start = (bf16[32,8192]{1,0:T(8,128)(2,1)S(1)}, bf16[32,8192]{1,0:T(8,128)(2,1)}, u32[]{:S(2)}) copy-start(bf16[32,8192]{1,0:T(8,128)(2,1)} %get-tuple-element.16) | copy-start | bytes 1572868
